TPU v7x, 32 devices: a whole 2x2x4 slice. The times are simulated.
32 devices in a mesh: parts: 2 (over y), expert: 4 (over z), dp: 4 (over x, core).
Axes of the slice: x: 2, y: 2, z: 4, core: 2. Of those that a mesh axis runs over, the one named last changes fastest.
Arguments:
- tokens: bfloat16 [256, 6144], P(('parts', 'expert'), 'dp'), parts along dimension 0, may hold values from -6 to 6
- cotangent: bfloat16 [256, 6144], P(('parts', 'expert'), 'dp'), parts along dimension 0, may hold values from -6 to 6
- w_gate: bfloat16 [4, 6144, 8192], P('parts', 'dp', 'expert'), parts along dimension 0, may hold values from -0.078125 to 0.078125
- w_up: bfloat16 [4, 6144, 8192], P('parts', 'dp', 'expert'), parts along dimension 0, may hold values from -0.078125 to 0.078125
- w_down: bfloat16 [4, 8192, 6144], P('parts', 'expert', 'dp'), parts along dimension 0, may hold values from -0.0625 to 0.0625
- gate_table: float32 [64, 2], replicated, may hold values from 0.1 to 1
- expert_ids: int32 [256, 2], P('parts'), parts along dimension 0, may hold values from 0 to 7, as said below
- gate_index: int32 [256], P('parts'), parts along dimension 0, may hold values from 0 to 63
- hot_ids: int32 [4], P('parts'), parts along dimension 0, may hold values from 0 to 7, as said below
Outputs:
- mixed: bfloat16 [256, 6144], P(('parts', 'expert'), 'dp'), parts along dimension 0
- grad_tokens: bfloat16 [256, 6144], P(('parts', 'expert'), 'dp'), parts along dimension 0
- grad_gate: bfloat16 [4, 6144, 8192], P('parts', 'dp', 'expert'), parts along dimension 0
- grad_up: bfloat16 [4, 6144, 8192], P('parts', 'dp', 'expert'), parts along dimension 0
- grad_down: bfloat16 [4, 8192, 6144], P('parts', 'expert', 'dp'), parts along dimension 0
There are 2 independent parts, one for each index of `parts`. A program takes and returns all parts, laid end to end along the dimension named above; an argument that names none is the same for every part. Nothing has to cross between parts.
Inputs may be any that keep to these rules, and one draw needn't show every extreme that they name: `expert_ids`: each row names two different experts. `hot_ids`: two different experts.
All inputs are finite; a program needn't handle non-finite values.
Results may differ from a plain program's by a relative error of at most 0.0095.
Values may be sent and summed in bfloat16 or wider, within the bound.
A program may use at most 192 MiB of HBM per device.

v0:
```python
import jax
import jax.numpy as jnp
from jax import lax
from jax.sharding import PartitionSpec as P


def routing_weight(gate_table, expert_ids, gate_index, hot_ids):
    table_rows = gate_table.shape[0]
    select = gate_index[:, None] == jnp.arange(table_rows, dtype=jnp.int32)[None, :]
    gates = jnp.sum(jnp.where(select[:, :, None], gate_table[None, :, :], jnp.float32(0.0)), axis=1)
    match = expert_ids[:, :, None] == hot_ids[None, None, :]
    return jnp.sum(jnp.where(match, gates[:, :, None], jnp.float32(0.0)), axis=1)


def local(tokens, cotangent, w_gate, w_up, w_down, gate_table, expert_ids, gate_index, hot_ids):
    rows_all, grad_all = (
        lax.all_gather(tokens, "expert", axis=0, tiled=True),
        lax.all_gather(cotangent, "expert", axis=0, tiled=True),
    )
    weight_all = routing_weight(gate_table, expert_ids, gate_index, hot_ids)
    gate_part = jnp.einsum("rd,hdf->hrf", rows_all, w_gate, preferred_element_type=jnp.float32)
    up_part = jnp.einsum("rd,hdf->hrf", rows_all, w_up, preferred_element_type=jnp.float32)
    pre_gate, pre_up = lax.psum((gate_part, up_part), "dp")
    weight = weight_all.T[:, :, None]
    sigma = jax.nn.sigmoid(pre_gate)
    product = (weight * pre_gate * sigma * pre_up).astype(jnp.bfloat16)
    mixed = lax.psum_scatter(
        jnp.einsum("hrf,hfd->rd", product, w_down, preferred_element_type=jnp.float32).astype(
            jnp.bfloat16
        ),
        "expert",
        scatter_dimension=0,
        tiled=True,
    )
    back_partial = jnp.einsum("rd,hfd->hrf", grad_all, w_down, preferred_element_type=jnp.float32)
    back = lax.psum(back_partial, "dp")
    scaled = weight * back
    d_gate = (scaled * pre_up * sigma * (1.0 + pre_gate * (1.0 - sigma))).astype(jnp.bfloat16)
    d_up = (scaled * pre_gate * sigma).astype(jnp.bfloat16)
    first_sum = jnp.einsum("hrf,hdf->rd", d_gate, w_gate, preferred_element_type=jnp.float32)
    grad_tokens = lax.psum_scatter(
        (
            first_sum + jnp.einsum("hrf,hdf->rd", d_up, w_up, preferred_element_type=jnp.float32)
        ).astype(jnp.bfloat16),
        "expert",
        scatter_dimension=0,
        tiled=True,
    )
    grad_gate = jnp.einsum(
        "rd,hrf->hdf", rows_all, d_gate, preferred_element_type=jnp.float32
    ).astype(jnp.bfloat16)
    grad_up = jnp.einsum("rd,hrf->hdf", rows_all, d_up, preferred_element_type=jnp.float32).astype(
        jnp.bfloat16
    )
    grad_down = jnp.einsum(
        "hrf,rd->hfd", product, grad_all, preferred_element_type=jnp.float32
    ).astype(jnp.bfloat16)
    return (mixed, grad_tokens, grad_gate, grad_up, grad_down)


def solution(mesh):
    placed = (
        P(("parts", "expert"), "dp"),
        P(("parts", "expert"), "dp"),
        P("parts", "dp", "expert"),
        P("parts", "dp", "expert"),
        P("parts", "expert", "dp"),
        P(),
        P("parts", None),
        P("parts"),
        P("parts"),
    )
    return jax.shard_map(
        local,
        mesh=mesh,
        in_specs=placed,
        out_specs=(
            P(("parts", "expert"), "dp"),
            P(("parts", "expert"), "dp"),
            P("parts", "dp", "expert"),
            P("parts", "dp", "expert"),
            P("parts", "expert", "dp"),
        ),
        check_vma=False,
    )
```

profile of v0, /device:TPU:0, one launch (start us, length us, event | category | flops | bytes accessed | tf_op | source)
XLA Modules:
  0.0 279.2 jit_solution(6965048452455706417)
XLA Ops:
  7.2 0.0 all-reduce.3.cloned.1.call-start
  7.2 0.0 copy-start
  7.2 16.6 %all_gather.6 = bf16[128,1536]{1,0:T(8,128)(2,1)S(1)} all-gather(bf16[32,1536]{1,0:T(8,128)(2,1)} %param.9), channel_id=1, replica_groups=mesh['parts'=2,'expert'=4,'dp'=4] {'expert'}, dimensions={0}, use_global_device_ids=true | all-gather | bytes 491520 | tf_op jit(solution)/shard_map/all_gather | solution.py:17
  23.8 7.9 %convolution_bitcast_fusion.1 = f32[2,128,2048]{1,2,0:T(8,128)} fusion(bf16[2,1536,2048]{2,1,0:T(8,128)(2,1)} %param.12, bf16[128,1536]{1,0:T(8,128)(2,1)S(1)} %all_gather.6), kind=kOutput, calls=%fused_computation.4 | convolution fusion | flops 1610612736 | bytes 15073280 | tf_op jit(solution)/shard_map/rd,hdf->hrf/dot_general | solution.py:22
  31.8 0.0 copy-done
  31.8 4.8 %convolution_bitcast_fusion.2 = f32[2,128,2048]{1,2,0:T(8,128)} fusion(bf16[2,1536,2048]{2,1,0:T(8,128)(2,1)S(1)} %copy-done, bf16[128,1536]{1,0:T(8,128)(2,1)S(1)} %all_gather.6), kind=kOutput, calls=%fused_computation.5 | convolution fusion | flops 1610612736 | bytes 15073280 | tf_op jit(solution)/shard_map/rd,hdf->hrf/dot_general | solution.py:21
  36.6 0.0 copy-done.1
  36.6 15.4 %all_gather.7 = bf16[128,1536]{1,0:T(8,128)(2,1)S(1)} all-gather(bf16[32,1536]{1,0:T(8,128)(2,1)S(1)} %copy-done.1), channel_id=1, replica_groups=mesh['parts'=2,'expert'=4,'dp'=4] {'expert'}, dimensions={0}, use_global_device_ids=true | all-gather | bytes 491520 | tf_op jit(solution)/shard_map/all_gather | solution.py:18
  52.0 0.0 slice-done.1
  52.0 0.0 copy-start.4
  52.0 0.0 copy-start.2
  52.0 0.0 copy-start.3
  52.0 0.0 copy-start.5
  52.1 4.8 %convolution_bitcast_fusion = f32[2,128,2048]{1,2,0:T(8,128)} fusion(bf16[2,2048,1536]{2,1,0:T(8,128)(2,1)S(1)} %bitcast.50, bf16[128,1536]{1,0:T(8,128)(2,1)S(1)} %all_gather.7), kind=kOutput, calls=%fused_computation.3 | convolution fusion | flops 1610612736 | bytes 15073280 | tf_op jit(solution)/shard_map/rd,hfd->hrf/dot_general | solution.py:35
  56.8 0.0 all-reduce.3.cloned.1.call-update
  56.8 0.2 reduce-scatter.5.cloned.1.call-start
  57.1 0.1 select_reduce_fusion
  57.2 0.1 fusion.9
  57.3 120.4 %all-reduce.3.cloned.1.call-done = (f32[2,128,2048]{1,2,0:T(8,128)}, f32[2,128,2048]{1,2,0:T(8,128)}, f32[2,128,2048]{1,2,0:T(8,128)}) async-done(((f32[2,128,2048]{1,2,0:T(8,128)}, f32[2,128,2048]{1,2,0:T(8,128)}, f32[2,128,2048]{1,2,0:T(8,128)}), (f32[2,128,2048]{1,2,0:T(8,128)}, f32[2,128,2048]{1,2,0:T(8,128)}, f32[2,128,2048]{1,2,0:T(8,128)})) %all-reduce.3.cloned.1.call-update) | async-done | bytes 6291472 | tf_op jit(solution)/shard_map/psum | solution.py:23
  177.7 4.2 %multiply_convert_fusion.1 = (bf16[2,128,2048]{1,2,0:T(8,128)(2,1)S(1)}, bf16[2,128,2048]{1,2,0:T(8,128)(2,1)S(1)}, bf16[2,128,2048]{1,2,0:T(8,128)(2,1)S(1)}) fusion(f32[2,128,2048]{1,2,0:T(8,128)} %get-tuple-element.16, f32[2,128,2048]{1,2,0:T(8,128)} %get-tuple-element.15, f32[2,128,2048]{1,2,0:T(8,128)} %get-tuple-element.17, f32[2,128]{1,0:T(2,128)S(1)} %bitcast.53), kind=kLoop, calls=%fused_computation.13 | loop fusion | flops 9437184 | bytes 9438208 | tf_op jit(solution)/shard_map/convert_element_type | solution.py:38
  181.9 9.8 %convolution_bitcast_fusion.3 = f32[128,1536]{1,0:T(8,128)} fusion(bf16[2,128,2048]{1,2,0:T(8,128)(2,1)S(1)} %get-tuple-element.19, bf16[2,1536,2048]{2,1,0:T(8,128)(2,1)} %param.12), kind=kOutput, calls=%fused_computation.6 | convolution fusion | flops 1610612736 | bytes 14417920 | tf_op jit(solution)/shard_map/hrf,hdf->rd/dot_general | solution.py:43
  191.7 6.6 %convert_bitcast_fusion = bf16[2,1536,2048]{1,2,0:T(8,128)(2,1)} fusion(bf16[2,128,2048]{1,2,0:T(8,128)(2,1)S(1)} %get-tuple-element.19, bf16[128,1536]{1,0:T(8,128)(2,1)S(1)} %all_gather.6), kind=kOutput, calls=%fused_computation | convolution fusion | flops 1616904192 | bytes 14024704 | tf_op jit(solution)/shard_map/rd,hrf->hdf/dot_general | solution.py:52
  198.2 6.6 %convert_bitcast_fusion.1 = bf16[2,1536,2048]{1,2,0:T(8,128)(2,1)} fusion(bf16[2,128,2048]{1,2,0:T(8,128)(2,1)S(1)} %get-tuple-element.18, bf16[128,1536]{1,0:T(8,128)(2,1)S(1)} %all_gather.6), kind=kOutput, calls=%fused_computation.1 | convolution fusion | flops 1616904192 | bytes 14024704 | tf_op jit(solution)/shard_map/rd,hrf->hdf/dot_general | solution.py:49
  204.8 6.2 %fusion.1 = bf16[128,1536]{1,0:T(8,128)(2,1)} fusion(f32[128,1536]{1,0:T(8,128)} %convolution_bitcast_fusion.3, bf16[2,128,2048]{1,2,0:T(8,128)(2,1)S(1)} %get-tuple-element.18, bf16[2,1536,2048]{2,1,0:T(8,128)(2,1)S(1)} %bitcast.52), kind=kOutput, calls=%fused_computation.10 | convolution fusion | flops 1611005952 | bytes 14811136 | tf_op jit(solution)/shard_map/hrf,hdf->rd/dot_general | solution.py:40
  211.0 0.0 reduce-scatter.5.cloned.1.call-update
  211.0 0.3 reduce-scatter.3.cloned.1.call-start
  211.3 16.6 %copy.28 = bf16[2,1536,2048]{2,1,0:T(8,128)(2,1)} copy(bf16[2,1536,2048]{1,2,0:T(8,128)(2,1)} %convert_bitcast_fusion.1) | data formatting | bytes 25165824
  227.9 16.6 %copy.29 = bf16[2,1536,2048]{2,1,0:T(8,128)(2,1)} copy(bf16[2,1536,2048]{1,2,0:T(8,128)(2,1)} %convert_bitcast_fusion) | data formatting | bytes 25165824
  244.6 7.2 %fusion.2 = bf16[128,1536]{1,0:T(8,128)(2,1)} fusion(bf16[2,128,2048]{1,2,0:T(8,128)(2,1)S(1)} %get-tuple-element.20, bf16[2,2048,1536]{2,1,0:T(8,128)(2,1)} %param.13), kind=kOutput, calls=%fused_computation.11 | convolution fusion | flops 1610809344 | bytes 14024704 | tf_op jit(solution)/shard_map/hrf,hfd->rd/dot_general | solution.py:28
  251.7 0.0 reduce-scatter.3.cloned.1.call-update
  251.7 6.6 %convolution_convert_fusion = bf16[2,2048,1536]{2,1,0:T(8,128)(2,1)} fusion(bf16[2,128,2048]{1,2,0:T(8,128)(2,1)S(1)} %get-tuple-element.20, bf16[128,1536]{1,0:T(8,128)(2,1)S(1)} %all_gather.7), kind=kOutput, calls=%fused_computation.2 | convolution fusion | flops 1616904192 | bytes 14024704 | tf_op jit(solution)/shard_map/hrf,rd->hfd/dot_general | solution.py:55
  258.3 14.4 %reduce-scatter.3.cloned.1.call-done = bf16[32,1536]{1,0:T(8,128)(2,1)} async-done(((bf16[128,1536]{1,0:T(8,128)(2,1)}), bf16[32,1536]{1,0:T(8,128)(2,1)}) %reduce-scatter.3.cloned.1.call-update) | async-done | bytes 98320 | tf_op jit(solution)/shard_map/reduce_scatter | solution.py:27
  (20 shorter events, 0.0 us)
Async XLA Ops:
  7.2 170.5 %all-reduce.3.cloned.1.call-start = ((), (), s32[]{:S(2)}) async-start(), calls=%async_computation.4 | async-start | bytes 12582912 | tf_op jit(solution)/shard_map/psum | solution.py:23
  7.2 24.5 %copy-start = (bf16[2,1536,2048]{2,1,0:T(8,128)(2,1)S(1)}, bf16[2,1536,2048]{2,1,0:T(8,128)(2,1)}, u32[]{:S(2)}) copy-start(bf16[2,1536,2048]{2,1,0:T(8,128)(2,1)} %param.11) | copy-start | bytes 37748740
  23.8 28.2 %slice-start = ((s8[12582912]{0:T(1024)(128)(4,1)}), s8[4194304]{0:T(1024)(128)(4,1)S(1)}, s32[]{:S(2)}) async-start(s8[12582912]{0:T(1024)(128)(4,1)} %bitcast.49), calls=%async_computation.5 | async-start | bytes 8388608
  23.8 28.2 %slice-start.1 = ((s8[12582912]{0:T(1024)(128)(4,1)}), s8[4194304]{0:T(1024)(128)(4,1)S(1)}, s32[]{:S(2)}) async-start(s8[12582912]{0:T(1024)(128)(4,1)} %bitcast.49), calls=%async_computation.6 | async-start | bytes 8388608
  31.8 4.8 %copy-start.1 = (bf16[32,1536]{1,0:T(8,128)(2,1)S(1)}, bf16[32,1536]{1,0:T(8,128)(2,1)}, u32[]{:S(2)}) copy-start(bf16[32,1536]{1,0:T(8,128)(2,1)} %param.10) | copy-start | bytes 294916
  31.8 20.2 %slice-start.2 = ((s8[12582912]{0:T(1024)(128)(4,1)}), s8[4194304]{0:T(1024)(128)(4,1)S(1)}, s32[]{:S(2)}) async-start(s8[12582912]{0:T(1024)(128)(4,1)} %bitcast.49), calls=%async_computation.7 | async-start | bytes 8388608
  52.0 5.1 %copy-start.4 = (s32[128]{0:T(128)S(1)}, s32[128]{0:T(128)}, u32[]{:S(2)}) copy-start(s32[128]{0:T(128)} %param.16) | copy-start | bytes 1540
  52.0 5.1 %copy-start.2 = (f32[64,2]{0,1:T(2,128)S(1)}, f32[64,2]{0,1:T(2,128)}, u32[]{:S(2)}) copy-start(f32[64,2]{0,1:T(2,128)} %param.14) | copy-start | bytes 1540
  52.0 5.2 %copy-start.3 = (s32[128,2]{0,1:T(2,128)S(1)}, s32[128,2]{0,1:T(2,128)}, u32[]{:S(2)}) copy-start(s32[128,2]{0,1:T(2,128)} %param.15) | copy-start | bytes 3076
  52.0 5.2 %copy-start.5 = (s32[2]{0:T(128)S(1)}, s32[2]{0:T(128)}, u32[]{:S(2)}) copy-start(s32[2]{0:T(128)} %param.17) | copy-start | bytes 28
  56.8 201.5 %reduce-scatter.5.cloned.1.call-start = ((), (), s32[]{:S(2)}) async-start(), calls=%async_computation.3 | async-start | bytes 491520 | tf_op jit(solution)/shard_map/reduce_scatter | solution.py:41
  191.7 13.1 %slice-start.3 = ((s8[12582912]{0:T(1024)(128)(4,1)}), s8[4194304]{0:T(1024)(128)(4,1)S(1)}, s32[]{:S(2)}) async-start(s8[12582912]{0:T(1024)(128)(4,1)} %bitcast.51), calls=%async_computation.8 | async-start | bytes 8388608
  191.7 13.1 %slice-start.4 = ((s8[12582912]{0:T(1024)(128)(4,1)}), s8[4194304]{0:T(1024)(128)(4,1)S(1)}, s32[]{:S(2)}) async-start(s8[12582912]{0:T(1024)(128)(4,1)} %bitcast.51), calls=%async_computation.9 | async-start | bytes 8388608
  198.2 6.6 %slice-start.5 = ((s8[12582912]{0:T(1024)(128)(4,1)}), s8[4194304]{0:T(1024)(128)(4,1)S(1)}, s32[]{:S(2)}) async-start(s8[12582912]{0:T(1024)(128)(4,1)} %bitcast.51), calls=%async_computation.10 | async-start | bytes 8388608
  211.0 61.6 %reduce-scatter.3.cloned.1.call-start = ((), (), s32[]{:S(2)}) async-start(), calls=%async_computation.2 | async-start | bytes 491520 | tf_op jit(solution)/shard_map/reduce_scatter | solution.py:27
Sparse Core Ops, SparseCore 0:
  57.0 120.6 all-reduce.2
  211.2 20.7 reduce-scatter.4
  251.9 20.7 reduce-scatter.2
where the time goes:
time: 280 us; the launch traced here: 279 us
  waiting for transfers between devices  135 us (48%)
  matrix products  60.4 us (22%)
  local copies, waits for them, and re-layouts  33.3 us (12%)
  blocking collectives  32 us (11%)
  between operations  13.9 us (5%)
  other arithmetic  4.36 us (2%)
    psum x1, waiting for transfers between devices, local(): pre_gate, pre_up = lax.psum((gate_part, up_part), 'dp')  120 us
    unnamed x26, local copies, waits for them, and re-layouts  33.3 us
    all_gather x1, blocking collectives, local(): lax.all_gather(tokens, 'expert', axis=0, tiled=True)  16.6 us
    all_gather x1, blocking collectives, local(): lax.all_gather(cotangent, 'expert', axis=0, tiled=True)  15.4 us
    reduce_scatter x1, waiting for transfers between devices, local(): lax.psum_scatter(jnp.einsum('hrf,hfd->rd', product, w_down, preferred_ele...  14.4 us
    dot_general x1, matrix products, local(): jnp.einsum('hrf,hdf->rd', d_up, w_up, preferred_element_type=jnp.float32)  9.81 us
    dot_general x1, matrix products, local(): jnp.einsum('rd,hdf->hrf', rows_all, w_up, preferred_element_type=jnp.floa...  7.95 us
    dot_general x1, matrix products, local(): jnp.einsum('hrf,hfd->rd', product, w_down, preferred_element_type=jnp.flo...  7.17 us
  transfers between devices with their start and end apart: 3, of which 2 were waited for; matrix products, arithmetic and copies ran while one was open for 17% of the time, Pallas kernels for 0%

commit v1 on v0

v1 whole, which is shorter than its diff:
```python
import functools

import jax
import jax.numpy as jnp
from jax import lax
from jax.experimental import pallas as pl
from jax.experimental.pallas import tpu as pltpu
from jax.sharding import PartitionSpec as P

MESH = pl.DeviceIdType.MESH
BF16, F32 = jnp.bfloat16, jnp.float32


def routing_weight(gate_table, expert_ids, gate_index, hot_ids):
    table_rows = gate_table.shape[0]
    select = gate_index[:, None] == jnp.arange(table_rows, dtype=jnp.int32)[None, :]
    gates = jnp.sum(jnp.where(select[:, :, None], gate_table[None, :, :], jnp.float32(0.0)), axis=1)
    match = expert_ids[:, :, None] == hot_ids[None, None, :]
    return jnp.sum(jnp.where(match, gates[:, :, None], jnp.float32(0.0)), axis=1)


def dot(a, b):
    return jnp.dot(a, b, preferred_element_type=F32)


def dot_nt(a, b):
    return lax.dot_general(a, b, (((1,), (1,)), ((), ())), preferred_element_type=F32)


def layer_kernel(
    n_expert, chunks, lead,
    tok_ref, cot_ref, wt_ref, wg_hbm, wu_hbm, wd_hbm,
    x_out, act_out, part_out,
    wg, wu, wd, xall, own, send1, recv1, send2, recv2, act, acc, part,
    w_sem, x_send, x_recv, s1, r1, s2, r2, s3, r3, out_sem, act_sem,
):
    rows, width = tok_ref.shape
    f = wg.shape[3]
    z = lax.axis_index("expert")
    dp = lax.axis_index("dp")
    mine = lax.rem(dp, 2)
    other = 1 - mine
    near = dp + 1 - 2 * mine
    far = lax.rem(dp + 2, 4)

    def load(k, h, s):
        cols = pl.ds(pl.multiple_of(s * f, f), f)
        if k == 2:
            src, dst = wd_hbm.at[h, cols, :], wd.at[h, s]
        else:
            src, dst = (wg_hbm, wu_hbm)[k].at[h, :, cols], (wg, wu)[k].at[h, s]
        return pltpu.make_async_copy(src, dst, w_sem.at[k, h, s])

    def load_gu(s, carry):
        for h in (other, mine):
            load(0, h, s).start()
            load(1, h, s).start()
        return carry

    def load_down(s, carry):
        for h in (other, mine):
            load(2, h, s).start()
        return carry

    def gather(k, step):
        peer = lax.rem(z + step, n_expert)
        mine_rows = pl.ds(pl.multiple_of(z * rows, rows), rows)
        return pltpu.make_async_remote_copy(
            src_ref=(tok_ref, cot_ref)[k],
            dst_ref=xall.at[k, mine_rows, :],
            send_sem=x_send.at[k, step],
            recv_sem=x_recv.at[k, step],
            device_id={"expert": peer},
            device_id_type=MESH,
        )

    barrier = pltpu.get_barrier_semaphore()

    def greet(step, carry):
        pl.semaphore_signal(
            barrier, inc=1, device_id={"expert": lax.rem(z + step, n_expert)}, device_id_type=MESH
        )
        return carry

    lax.fori_loop(0, lead, load_gu, 0)
    lax.fori_loop(1, n_expert, greet, 0)
    pl.semaphore_signal(barrier, inc=1, device_id={"dp": near}, device_id_type=MESH)
    pl.semaphore_signal(barrier, inc=1, device_id={"dp": far}, device_id_type=MESH)
    pl.semaphore_wait(barrier, n_expert + 1)

    for k in range(2):
        def send_rows(step, carry, k=k):
            gather(k, step).start()
            return carry
        lax.fori_loop(1, n_expert, send_rows, 0)

    def later(s, carry):
        load_down(s, 0)

        @pl.when(s + lead < chunks)
        def _():
            load_gu(s + lead, 0)
        return carry

    lax.fori_loop(0, chunks, later, 0)
    own_rows = pl.ds(pl.multiple_of(z * rows, rows), rows)
    xall[0, own_rows, :] = tok_ref[...]
    xall[1, own_rows, :] = cot_ref[...]
    acc[...] = jnp.zeros_like(acc)

    def arrive(k):
        def body(step, carry):
            gather(k, step).wait_recv()
            return carry
        lax.fori_loop(1, n_expert, body, 0)
        pltpu.make_async_copy(xall.at[k], x_out.at[k], out_sem.at[k]).start()

    span = (pl.ds(0, 2), pl.ds(2, 1))

    def to_near(g, s):
        return pltpu.make_async_remote_copy(
            src_ref=send1.at[s, span[g]], dst_ref=recv1.at[s, span[g]],
            send_sem=s1.at[g, s], recv_sem=r1.at[g, s],
            device_id={"dp": near}, device_id_type=MESH,
        )

    def to_far(g, s):
        return pltpu.make_async_remote_copy(
            src_ref=send2.at[s, span[g]], dst_ref=recv2.at[s, span[g]],
            send_sem=s2.at[g, s], recv_sem=r2.at[g, s],
            device_id={"dp": far}, device_id_type=MESH,
        )

    def act_to_near(h, s):
        return pltpu.make_async_remote_copy(
            src_ref=act.at[h, s], dst_ref=act.at[h, s],
            send_sem=s3.at[s], recv_sem=r3.at[s],
            device_id={"dp": near}, device_id_type=MESH,
        )

    def act_copy(h, s):
        cols = pl.ds(pl.multiple_of(s * f, f), f)
        return pltpu.make_async_copy(act.at[h, s], act_out.at[h, :, :, cols], act_sem.at[h, s])

    def gate_up(s):
        for k, w in ((0, wg), (1, wu)):
            load(k, other, s).wait()
            send1[s, k] = dot(xall[0], w[other, s]).astype(BF16)
        to_near(0, s).start()
        for k, w in ((0, wg), (1, wu)):
            load(k, mine, s).wait()
            own[s, k] = dot(xall[0], w[mine, s])

    def back(s):
        load(2, other, s).wait()
        send1[s, 2] = dot_nt(xall[1], wd[other, s]).astype(BF16)
        to_near(1, s).start()
        load(2, mine, s).wait()
        own[s, 2] = dot_nt(xall[1], wd[mine, s])

    def pair(g, s):
        to_near(g, s).wait_recv()
        for k in ((0, 1), (2,))[g]:
            both = own[s, k] + recv1[s, k].astype(F32)
            own[s, k] = both
            send2[s, k] = both.astype(BF16)
        to_far(g, s).start()

    arrive(0)

    def first(s, carry):
        @pl.when(s < chunks)
        def _():
            gate_up(s)

        @pl.when((s >= 1) & (s <= chunks))
        def _():
            pair(0, s - 1)

        @pl.when(s == lead)
        def _():
            arrive(1)

        @pl.when((s >= lead) & (s < chunks + lead))
        def _():
            back(s - lead)

        @pl.when(s >= lead + 1)
        def _():
            pair(1, s - lead - 1)
        return carry

    lax.fori_loop(0, chunks + lead + 1, first, 0)

    def project(h, s):
        acc[0] += dot(act[h, s, 0], wd[h, s])
        acc[1] += dot_nt(act[h, s, 1], wg[h, s]) + dot_nt(act[h, s, 2], wu[h, s])

    def second(s, carry):
        @pl.when(s < chunks)
        def _():
            to_far(0, s).wait_recv()
            to_far(1, s).wait_recv()
            weight = wt_ref[mine]
            gate = own[s, 0] + recv2[s, 0].astype(F32)
            up = own[s, 1] + recv2[s, 1].astype(F32)
            scaled = weight * (own[s, 2] + recv2[s, 2].astype(F32))
            sigma = jax.nn.sigmoid(gate)
            silu = gate * sigma
            act[mine, s, 0] = (weight * silu * up).astype(BF16)
            act[mine, s, 1] = (scaled * up * (sigma * (1.0 + gate * (1.0 - sigma)))).astype(BF16)
            act[mine, s, 2] = (scaled * silu).astype(BF16)
            act_to_near(mine, s).start()
            act_copy(mine, s).start()
            project(mine, s)

        @pl.when(s >= 1)
        def _():
            act_to_near(other, s - 1).wait_recv()
            act_copy(other, s - 1).start()
            project(other, s - 1)
        return carry

    lax.fori_loop(0, chunks + 1, second, 0)

    part[:, :width] = acc[0].astype(BF16)
    part[:, width:] = acc[1].astype(BF16)
    last = pltpu.make_async_copy(part, part_out, out_sem.at[2])
    last.start()

    def drain(s, carry):
        for g in range(2):
            to_near(g, s).wait_send()
            to_far(g, s).wait_send()
        act_to_near(mine, s).wait_send()
        for h in range(2):
            act_copy(h, s).wait()
        return carry

    lax.fori_loop(0, chunks, drain, 0)

    def drain_rows(step, carry):
        for k in range(2):
            gather(k, step).wait_send()
        return carry

    lax.fori_loop(1, n_expert, drain_rows, 0)
    for k in range(2):
        pltpu.make_async_copy(xall.at[k], x_out.at[k], out_sem.at[k]).wait()
    last.wait()


def grads_kernel(x_ref, act_ref, gg_ref, gu_ref, gd_ref, tok_t):
    @pl.when((pl.program_id(0) == 0) & (pl.program_id(1) == 0))
    def _():
        tok_t[...] = x_ref[0].T

    gg_ref[0] = dot(tok_t[...], act_ref[0, 1]).astype(BF16)
    gu_ref[0] = dot(tok_t[...], act_ref[0, 2]).astype(BF16)
    gd_ref[0] = dot(act_ref[0, 0].T, x_ref[1]).astype(BF16)


def local(n_expert, tokens, cotangent, w_gate, w_up, w_down, gate_table, expert_ids, gate_index, hot_ids):
    rows, width = tokens.shape
    hot, _, hidden = w_gate.shape
    total = rows * n_expert
    f = min(256, hidden)
    chunks = hidden // f
    lead = chunks // 2
    weight = routing_weight(gate_table, expert_ids, gate_index, hot_ids).T[:, :, None]
    vmem, anywhere = pl.BlockSpec(memory_space=pltpu.VMEM), pl.BlockSpec(memory_space=pl.ANY)
    dma = pltpu.SemaphoreType.DMA
    x_all, acts, partial = pl.pallas_call(
        functools.partial(layer_kernel, n_expert, chunks, lead),
        out_shape=(
            jax.ShapeDtypeStruct((2, total, width), BF16),
            jax.ShapeDtypeStruct((hot, 3, total, hidden), BF16),
            jax.ShapeDtypeStruct((total, 2 * width), BF16),
        ),
        in_specs=[vmem, vmem, vmem, anywhere, anywhere, anywhere],
        out_specs=(anywhere, anywhere, anywhere),
        scratch_shapes=[
            pltpu.VMEM((hot, chunks, width, f), BF16),
            pltpu.VMEM((hot, chunks, width, f), BF16),
            pltpu.VMEM((hot, chunks, f, width), BF16),
            pltpu.VMEM((2, total, width), BF16),
            pltpu.VMEM((chunks, 3, total, f), F32),
            pltpu.VMEM((chunks, 3, total, f), BF16),
            pltpu.VMEM((chunks, 3, total, f), BF16),
            pltpu.VMEM((chunks, 3, total, f), BF16),
            pltpu.VMEM((chunks, 3, total, f), BF16),
            pltpu.VMEM((hot, chunks, 3, total, f), BF16),
            pltpu.VMEM((2, total, width), F32),
            pltpu.VMEM((total, 2 * width), BF16),
            dma((3, hot, chunks)),
            dma((2, n_expert)),
            dma((2, n_expert)),
            dma((2, chunks)),
            dma((2, chunks)),
            dma((2, chunks)),
            dma((2, chunks)),
            dma((chunks,)),
            dma((chunks,)),
            dma((3,)),
            dma((hot, chunks)),
        ],
        compiler_params=pltpu.CompilerParams(
            collective_id=0, has_side_effects=True, vmem_limit_bytes=60 * 1024 * 1024
        ),
    )(tokens, cotangent, weight, w_gate, w_up, w_down)
    reduced = lax.psum_scatter(partial, "expert", scatter_dimension=0, tiled=True)
    grad_gate, grad_up, grad_down = pl.pallas_call(
        grads_kernel,
        grid=(hot, chunks),
        out_shape=(
            jax.ShapeDtypeStruct((hot, width, hidden), BF16),
            jax.ShapeDtypeStruct((hot, width, hidden), BF16),
            jax.ShapeDtypeStruct((hot, hidden, width), BF16),
        ),
        in_specs=[
            pl.BlockSpec((2, total, width), lambda h, s: (0, 0, 0)),
            pl.BlockSpec((1, 3, total, f), lambda h, s: (h, 0, 0, s)),
        ],
        out_specs=(
            pl.BlockSpec((1, width, f), lambda h, s: (h, 0, s)),
            pl.BlockSpec((1, width, f), lambda h, s: (h, 0, s)),
            pl.BlockSpec((1, f, width), lambda h, s: (h, s, 0)),
        ),
        scratch_shapes=[pltpu.VMEM((width, total), BF16)],
        cost_estimate=pl.CostEstimate(
            flops=6 * hot * total * width * hidden,
            bytes_accessed=6 * hot * width * hidden,
            transcendentals=0,
        ),
        compiler_params=pltpu.CompilerParams(vmem_limit_bytes=48 * 1024 * 1024),
    )(x_all, acts)
    return reduced[:, :width], reduced[:, width:], grad_gate, grad_up, grad_down


def solution(mesh):
    placed = (
        P(("parts", "expert"), "dp"),
        P(("parts", "expert"), "dp"),
        P("parts", "dp", "expert"),
        P("parts", "dp", "expert"),
        P("parts", "expert", "dp"),
        P(),
        P("parts", None),
        P("parts"),
        P("parts"),
    )
    return jax.shard_map(
        functools.partial(local, mesh.shape["expert"]),
        mesh=mesh,
        in_specs=placed,
        out_specs=(
            P(("parts", "expert"), "dp"),
            P(("parts", "expert"), "dp"),
            P("parts", "dp", "expert"),
            P("parts", "dp", "expert"),
            P("parts", "expert", "dp"),
        ),
        check_vma=False,
    )
```

time: 280 us -> 108 us (0.39)
  waiting for transfers between devices: 135 us -> 9.21 us
  Pallas kernels: 0 us -> 76.6 us
  matrix products: 60.4 us -> 0 us
  blocking collectives: 32 us -> 0 us
  local copies, waits for them, and re-layouts: 33.3 us -> 5.44 us
    psum x1 -> x0, waiting for transfers between devices: 120 us -> none  [local(): pre_gate, pre_up = lax.psum((gate_part, up_part), 'dp')]
    pallas_call x0 -> x2, Pallas kernels: none -> 76.6 us  [the longest x1 60.1 us: local(): pl.pallas_call(functools.partial(layer_kernel, n_expert, chunks, lead), o...]
    dot_general x9 -> x0, matrix products: 60.4 us -> none  [the longest x1 9.81 us: local(): jnp.einsum('hrf,hdf->rd', d_up, w_up, preferred_element_type=jnp.float32)]
    all_gather x2 -> x0, blocking collectives: 32 us -> none  [the longest x1 16.6 us: local(): lax.all_gather(tokens, 'expert', axis=0, tiled=True)]
    unnamed x26 -> x4, local copies, waits for them, and re-layouts: 33.3 us -> 3.02 us
    reduce_scatter x2 -> x1, waiting for transfers between devices: 14.4 us -> 9.2 us  [local(): lax.psum_scatter(partial, 'expert', scatter_dimension=0, tiled=True)]
    convert_element_type x1 -> x0, other arithmetic: 4.17 us -> none  [local(): (scaled * pre_up * sigma * (1.0 + pre_gate * (1.0 - sigma))).astype(jnp.b...]
  transfers between devices with their start and end apart: 3 -> 1, of which waited for: 2 -> 1; matrix products, arithmetic and copies ran while one was open for 17% -> 0% of each run, Pallas kernels for 0% -> 15%
where the time goes in v1:
time: 108 us
  Pallas kernels  76.6 us (71%)
  between operations  14 us (13%)
  waiting for transfers between devices  9.21 us (9%)
  local copies, waits for them, and re-layouts  5.44 us (5%)
  other arithmetic  2.2 us (2%)
    pallas_call x1, Pallas kernels, local(): pl.pallas_call(functools.partial(layer_kernel, n_expert, chunks, lead), o...  60.1 us
    pallas_call x1, Pallas kernels, local(): pl.pallas_call(grads_kernel, grid=(hot, chunks), out_shape=(jax.ShapeDtyp...  16.5 us
    reduce_scatter x1, waiting for transfers between devices, local(): lax.psum_scatter(partial, 'expert', scatter_dimension=0, tiled=True)  9.2 us
    unnamed x4, local copies, waits for them, and re-layouts  3.02 us
  transfers between devices with their start and end apart: 1, of which 1 were waited for; matrix products, arithmetic and copies ran while one was open for 0% of the time, Pallas kernels for 15%

profile of v1, /device:TPU:0, one launch (start us, length us, event | category | flops | bytes accessed | tf_op | source)
XLA Modules:
  0.0 107.5 jit_solution(1334187537047651845)
XLA Ops:
  7.2 0.0 reduce-scatter.2.cloned.1.call-start
  7.2 0.7 iota_compare_fusion
  7.9 0.8 select_reduce_fusion
  8.6 0.8 fusion
  9.4 0.8 copy.19.wt_ref
  10.2 60.1 %shard_map.128 = (bf16[2,128,1536]{2,1,0:T(8,128)(2,1)}, bf16[2,3,128,2048]{3,2,1,0:T(8,128)(2,1)}, bf16[128,3072]{1,0:T(8,128)(2,1)}) custom-call(bf16[32,1536]{1,0:T(8,128)(2,1)} %tok_ref.1, bf16[32,1536]{1,0:T(8,128)(2,1)} %cot_ref.1, f32[2,128,1]{2,1,0:T(8,128)} %copy.19.wt_ref, bf16[2,1536,2048]{2,1,0:T(8,128)(2,1)} %wg_hbm.1, ...), custom_call_target="tpu_custom_call" | custom-call | tf_op jit(solution)/shard_map/pallas_call | solution.py:273
  70.3 0.0 reduce-scatter.2.cloned.1.call-update
  70.3 0.0 copy-start
  70.3 1.9 %copy-done = bf16[2,3,128,2048]{3,2,1,0:T(8,128)(2,1)S(1)} copy-done((bf16[2,3,128,2048]{3,2,1,0:T(8,128)(2,1)S(1)}, bf16[2,3,128,2048]{3,2,1,0:T(8,128)(2,1)}, u32[]{:S(2)}) %copy-start) | copy-done | bytes 3145752
  72.2 0.0 copy-start.1
  72.2 1.1 %copy-done.1 = bf16[2,128,1536]{2,1,0:T(8,128)(2,1)S(1)} copy-done((bf16[2,128,1536]{2,1,0:T(8,128)(2,1)S(1)}, bf16[2,128,1536]{2,1,0:T(8,128)(2,1)}, u32[]{:S(2)}) %copy-start.1) | copy-done | bytes 786456
  73.3 16.5 %shard_map.129 = (bf16[2,1536,2048]{2,1,0:T(8,128)(2,1)}, bf16[2,1536,2048]{2,1,0:T(8,128)(2,1)}, bf16[2,2048,1536]{2,1,0:T(8,128)(2,1)}) custom-call(bf16[2,128,1536]{2,1,0:T(8,128)(2,1)S(1)} %copy-done.1, bf16[2,3,128,2048]{3,2,1,0:T(8,128)(2,1)S(1)} %copy-done), custom_call_target="tpu_custom_call" | custom-call | flops 4831838208 | bytes 37748736 | tf_op jit(solution)/shard_map/pallas_call | solution.py:312
  89.9 9.2 %reduce-scatter.2.cloned.1.call-done = bf16[32,3072]{1,0:T(8,128)(2,1)} async-done(((bf16[128,3072]{1,0:T(8,128)(2,1)}), bf16[32,3072]{1,0:T(8,128)(2,1)}) %reduce-scatter.2.cloned.1.call-update) | async-done | bytes 196624 | tf_op jit(solution)/shard_map/reduce_scatter | solution.py:311
  99.1 1.6 %fusion.1 = (bf16[32,1536]{1,0:T(8,128)(2,1)}, bf16[32,1536]{1,0:T(8,128)(2,1)}) fusion(bf16[32,3072]{1,0:T(8,128)(2,1)} %reduce-scatter.2.cloned.1.call-done), kind=kLoop, calls=%fused_computation.4 | loop fusion | bytes 393216 | tf_op jit(solution)/shard_map/slice | solution.py:337
Async XLA Ops:
  7.2 91.9 %reduce-scatter.2.cloned.1.call-start = ((), (), s32[]{:S(2)}) async-start(), calls=%async_computation.1 | async-start | bytes 983040 | tf_op jit(solution)/shard_map/reduce_scatter | solution.py:311
  70.3 1.9 %copy-start = (bf16[2,3,128,2048]{3,2,1,0:T(8,128)(2,1)S(1)}, bf16[2,3,128,2048]{3,2,1,0:T(8,128)(2,1)}, u32[]{:S(2)}) copy-start(bf16[2,3,128,2048]{3,2,1,0:T(8,128)(2,1)} %get-tuple-element.13.act_ref) | copy-start | bytes 9437188
  72.2 1.1 %copy-start.1 = (bf16[2,128,1536]{2,1,0:T(8,128)(2,1)S(1)}, bf16[2,128,1536]{2,1,0:T(8,128)(2,1)}, u32[]{:S(2)}) copy-start(bf16[2,128,1536]{2,1,0:T(8,128)(2,1)} %get-tuple-element.12.x_ref) | copy-start | bytes 2359300
Sparse Core Ops, SparseCore 0:
  70.4 28.5 reduce-scatter.1

commit v2 on v1

--- a/solution.py
+++ b/solution.py
@@ -11,14 +11,6 @@
 BF16, F32 = jnp.bfloat16, jnp.float32
 
 
-def routing_weight(gate_table, expert_ids, gate_index, hot_ids):
-    table_rows = gate_table.shape[0]
-    select = gate_index[:, None] == jnp.arange(table_rows, dtype=jnp.int32)[None, :]
-    gates = jnp.sum(jnp.where(select[:, :, None], gate_table[None, :, :], jnp.float32(0.0)), axis=1)
-    match = expert_ids[:, :, None] == hot_ids[None, None, :]
-    return jnp.sum(jnp.where(match, gates[:, :, None], jnp.float32(0.0)), axis=1)
-
-
 def dot(a, b):
     return jnp.dot(a, b, preferred_element_type=F32)
 
@@ -29,11 +21,12 @@
 
 def layer_kernel(
     n_expert, chunks, lead,
-    tok_ref, cot_ref, wt_ref, wg_hbm, wu_hbm, wd_hbm,
-    x_out, act_out, part_out,
-    wg, wu, wd, xall, own, send1, recv1, send2, recv2, act, acc, part,
-    w_sem, x_send, x_recv, s1, r1, s2, r2, s3, r3, out_sem, act_sem,
+    tok_ref, cot_ref, table_ref, ids_ref, index_ref, hot_ref, wg_hbm, wu_hbm, wd_hbm,
+    x_out, act_out, *rest,
 ):
+    part_out, rest = rest[:n_expert], rest[n_expert:]
+    (wg, wu, wd, xall, own, send1, recv1, send2, recv2, act, acc, part, wt,
+     w_sem, x_send, x_recv, s1, r1, s2, r2, s3, r3, out_sem, act_sem, part_sem) = rest
     rows, width = tok_ref.shape
     f = wg.shape[3]
     z = lax.axis_index("expert")
@@ -108,6 +101,19 @@
     xall[1, own_rows, :] = cot_ref[...]
     acc[...] = jnp.zeros_like(acc)
 
+    slots, total = table_ref.shape[1], index_ref.shape[1]
+    select = lax.broadcasted_iota(jnp.int32, (slots, total), 0) == index_ref[...]
+    even = lax.rem(lax.broadcasted_iota(jnp.int32, (8, slots), 0), 2) == 0
+    table = jnp.where(even, table_ref[0:1, :], table_ref[1:2, :]).T
+    first_gate, second_gate = (
+        jnp.sum(jnp.where(select, table[:, k:k + 1], 0.0), axis=0, keepdims=True) for k in range(2)
+    )
+    hot = jnp.where(mine == 0, hot_ref[:, 0:1], hot_ref[:, 1:2])
+    weight_row = jnp.where(ids_ref[0:1, :] == hot, first_gate, 0.0) + jnp.where(
+        ids_ref[1:2, :] == hot, second_gate, 0.0
+    )
+    wt[...] = jnp.broadcast_to(weight_row, (8, total)).T[:, 0:1]
+
     def arrive(k):
         def body(step, carry):
             gather(k, step).wait_recv()
@@ -201,7 +207,7 @@
         def _():
             to_far(0, s).wait_recv()
             to_far(1, s).wait_recv()
-            weight = wt_ref[mine]
+            weight = wt[...]
             gate = own[s, 0] + recv2[s, 0].astype(F32)
             up = own[s, 1] + recv2[s, 1].astype(F32)
             scaled = weight * (own[s, 2] + recv2[s, 2].astype(F32))
@@ -225,8 +231,11 @@
 
     part[:, :width] = acc[0].astype(BF16)
     part[:, width:] = acc[1].astype(BF16)
-    last = pltpu.make_async_copy(part, part_out, out_sem.at[2])
-    last.start()
+    copies = []
+    for step in range(n_expert):
+        to_rows = pl.ds(pl.multiple_of(lax.rem(z + step, n_expert) * rows, rows), rows)
+        copies.append(pltpu.make_async_copy(part.at[to_rows, :], part_out[step], part_sem.at[step]))
+        copies[-1].start()
 
     def drain(s, carry):
         for g in range(2):
@@ -247,7 +256,8 @@
     lax.fori_loop(1, n_expert, drain_rows, 0)
     for k in range(2):
         pltpu.make_async_copy(xall.at[k], x_out.at[k], out_sem.at[k]).wait()
-    last.wait()
+    for copy in copies:
+        copy.wait()
 
 
 def grads_kernel(x_ref, act_ref, gg_ref, gu_ref, gd_ref, tok_t):
@@ -267,18 +277,16 @@
     f = min(256, hidden)
     chunks = hidden // f
     lead = chunks // 2
-    weight = routing_weight(gate_table, expert_ids, gate_index, hot_ids).T[:, :, None]
     vmem, anywhere = pl.BlockSpec(memory_space=pltpu.VMEM), pl.BlockSpec(memory_space=pl.ANY)
     dma = pltpu.SemaphoreType.DMA
-    x_all, acts, partial = pl.pallas_call(
+    x_all, acts, *blocks = pl.pallas_call(
         functools.partial(layer_kernel, n_expert, chunks, lead),
         out_shape=(
             jax.ShapeDtypeStruct((2, total, width), BF16),
             jax.ShapeDtypeStruct((hot, 3, total, hidden), BF16),
-            jax.ShapeDtypeStruct((total, 2 * width), BF16),
-        ),
-        in_specs=[vmem, vmem, vmem, anywhere, anywhere, anywhere],
-        out_specs=(anywhere, anywhere, anywhere),
+        ) + (jax.ShapeDtypeStruct((rows, 2 * width), BF16),) * n_expert,
+        in_specs=[vmem] * 6 + [anywhere] * 3,
+        out_specs=(anywhere,) * (2 + n_expert),
         scratch_shapes=[
             pltpu.VMEM((hot, chunks, width, f), BF16),
             pltpu.VMEM((hot, chunks, width, f), BF16),
@@ -292,6 +300,7 @@
             pltpu.VMEM((hot, chunks, 3, total, f), BF16),
             pltpu.VMEM((2, total, width), F32),
             pltpu.VMEM((total, 2 * width), BF16),
+            pltpu.VMEM((total, 1), F32),
             dma((3, hot, chunks)),
             dma((2, n_expert)),
             dma((2, n_expert)),
@@ -301,17 +310,25 @@
             dma((2, chunks)),
             dma((chunks,)),
             dma((chunks,)),
-            dma((3,)),
+            dma((2,)),
             dma((hot, chunks)),
+            dma((n_expert,)),
         ],
         compiler_params=pltpu.CompilerParams(
             collective_id=0, has_side_effects=True, vmem_limit_bytes=60 * 1024 * 1024
         ),
-    )(tokens, cotangent, weight, w_gate, w_up, w_down)
-    reduced = lax.psum_scatter(partial, "expert", scatter_dimension=0, tiled=True)
+    )(
+        tokens, cotangent, gate_table.T, expert_ids.T,
+        gate_index.reshape(1, total), hot_ids.reshape(1, hot), w_gate, w_up, w_down,
+    )
+    arrived = [
+        lax.ppermute(block, "expert", [(i, (i + step) % n_expert) for i in range(n_expert)])
+        for step, block in enumerate(blocks) if step > 0
+    ]
+    wide = min(512, hidden)
     grad_gate, grad_up, grad_down = pl.pallas_call(
         grads_kernel,
-        grid=(hot, chunks),
+        grid=(hot, hidden // wide),
         out_shape=(
             jax.ShapeDtypeStruct((hot, width, hidden), BF16),
             jax.ShapeDtypeStruct((hot, width, hidden), BF16),
@@ -319,12 +336,12 @@
         ),
         in_specs=[
             pl.BlockSpec((2, total, width), lambda h, s: (0, 0, 0)),
-            pl.BlockSpec((1, 3, total, f), lambda h, s: (h, 0, 0, s)),
+            pl.BlockSpec((1, 3, total, wide), lambda h, s: (h, 0, 0, s)),
         ],
         out_specs=(
-            pl.BlockSpec((1, width, f), lambda h, s: (h, 0, s)),
-            pl.BlockSpec((1, width, f), lambda h, s: (h, 0, s)),
-            pl.BlockSpec((1, f, width), lambda h, s: (h, s, 0)),
+            pl.BlockSpec((1, width, wide), lambda h, s: (h, 0, s)),
+            pl.BlockSpec((1, width, wide), lambda h, s: (h, 0, s)),
+            pl.BlockSpec((1, wide, width), lambda h, s: (h, s, 0)),
         ),
         scratch_shapes=[pltpu.VMEM((width, total), BF16)],
         cost_estimate=pl.CostEstimate(
@@ -332,9 +349,15 @@
             bytes_accessed=6 * hot * width * hidden,
             transcendentals=0,
         ),
-        compiler_params=pltpu.CompilerParams(vmem_limit_bytes=48 * 1024 * 1024),
+        compiler_params=pltpu.CompilerParams(vmem_limit_bytes=60 * 1024 * 1024),
     )(x_all, acts)
-    return reduced[:, :width], reduced[:, width:], grad_gate, grad_up, grad_down
+    mixed, grad_tokens = (
+        functools.reduce(
+            jnp.add, [block[:, half].astype(F32) for block in [blocks[0]] + arrived]
+        ).astype(BF16)
+        for half in (slice(0, width), slice(width, None))
+    )
+    return mixed, grad_tokens, grad_gate, grad_up, grad_down
 
 
 def solution(mesh):

time: 108 us -> 86.1 us (0.80)
  between operations: 14 us -> 0.67 us
  waiting for transfers between devices: 9.21 us -> 0.01 us
  starting transfers between devices: 0.04 us -> 9.17 us
  local copies, waits for them, and re-layouts: 5.44 us -> 0.01 us
  other arithmetic: 2.2 us -> 0.77 us
  Pallas kernels: 76.6 us -> 75.3 us
    reduce_scatter x1 -> x0, waiting for transfers between devices: 9.2 us -> none  [local(): lax.psum_scatter(partial, 'expert', scatter_dimension=0, tiled=True)]
    ppermute x0 -> x3, starting transfers between devices: none -> 9.17 us  [local(): lax.ppermute(block, 'expert', [(i, (i + step) % n_expert) for i in range(...]
    unnamed x4 -> x2, local copies, waits for them, and re-layouts: 3.02 us -> 0.01 us
    slice x1 -> x0, local copies, waits for them, and re-layouts: 1.63 us -> none  [local(): reduced[:, width:]]
    reduce_sum x2 -> x0, other arithmetic: 1.53 us -> none  [the longest x1 0.77 us: routing_weight(): jnp.sum(jnp.where(select[:, :, None], gate_table[None, :, :], jnp.float32...]
    pallas_call x1, Pallas kernels: 16.5 us -> 15.2 us  [local(): pl.pallas_call(grads_kernel, grid=(hot, hidden // wide), out_shape=(jax.S...]
  transfers between devices with their start and end apart: 1 -> 3, of which waited for: 1 -> 0; matrix products, arithmetic and copies ran while one was open for 0% -> 0% of each run, Pallas kernels for 15% -> 18%
where the time goes in v2:
time: 86.1 us; the launch traced here: 85.9 us
  Pallas kernels  75.3 us (87%)
  starting transfers between devices  9.17 us (11%)
    pallas_call x1, Pallas kernels, local(): pl.pallas_call(functools.partial(layer_kernel, n_expert, chunks, lead), o...  60.1 us
    pallas_call x1, Pallas kernels, local(): pl.pallas_call(grads_kernel, grid=(hot, hidden // wide), out_shape=(jax.S...  15.2 us
    ppermute x3, starting transfers between devices, local(): lax.ppermute(block, 'expert', [(i, (i + step) % n_expert) for i in range(...  9.17 us
  transfers between devices with their start and end apart: 3, of which 0 were waited for; matrix products, arithmetic and copies ran while one was open for 0% of the time, Pallas kernels for 18%

profile of v2, /device:TPU:0, one launch (start us, length us, event | category | flops | bytes accessed | tf_op | source)
XLA Modules:
  0.0 85.9 jit_solution(4936334862307339580)
XLA Ops:
  0.6 60.1 %shard_map.128 = (bf16[2,128,1536]{2,1,0:T(8,128)(2,1)}, bf16[2,3,128,2048]{3,2,1,0:T(8,128)(2,1)}, bf16[32,3072]{1,0:T(8,128)(2,1)}, bf16[32,3072]{1,0:T(8,128)...) custom-call(bf16[32,1536]{1,0:T(8,128)(2,1)} %tok_ref.1, bf16[32,1536]{1,0:T(8,128)(2,1)} %cot_ref.1, ...), custom_call_target="tpu_custom_call" | custom-call | tf_op jit(solution)/shard_map/pallas_call | solution.py:282
  60.8 0.0 copy-start
  60.8 6.2 %collective-permute-start = (bf16[32,3072]{1,0:T(8,128)(2,1)}, bf16[32,3072]{1,0:T(8,128)(2,1)S(1)}, u32[]{:S(2)}, u32[]{:S(2)}) collective-permute-start(bf16[32,3072]{1,0:T(8,128)(2,1)} %get-tuple-element.15), channel_id=1, source_target_pairs={{0,4},{4,8},{8,12},{12,0},{1,5},{5,9},{9,13},{13,1},{2,6},{6,10},{... | collective-permute-start | bytes 589832 | tf_op jit(solution)/shard_map/ppermute | solution.py:325
  67.0 2.9 %collective-permute-start.1 = (bf16[32,3072]{1,0:T(8,128)(2,1)}, bf16[32,3072]{1,0:T(8,128)(2,1)S(1)}, u32[]{:S(2)}, u32[]{:S(2)}) collective-permute-start(bf16[32,3072]{1,0:T(8,128)(2,1)} %get-tuple-element.16), channel_id=1, source_target_pairs={{0,8},{4,12},{8,0},{12,4},{1,9},{5,13},{9,1},{13,5},{2,10},{6,14},... | collective-permute-start | bytes 589832 | tf_op jit(solution)/shard_map/ppermute | solution.py:325
  69.9 0.0 collective-permute-start.2
  69.9 15.2 %shard_map.129 = (bf16[2,1536,2048]{2,1,0:T(8,128)(2,1)}, bf16[2,1536,2048]{2,1,0:T(8,128)(2,1)}, bf16[2,2048,1536]{2,1,0:T(8,128)(2,1)}) custom-call(bf16[2,128,1536]{2,1,0:T(8,128)(2,1)} %get-tuple-element.18.x_ref, bf16[2,3,128,2048]{3,2,1,0:T(8,128)(2,1)} %get-tuple-element.19.act_ref), custom_call_target="tpu_custom_call" | custom-call | flops 4831838208 | bytes 37748736 | tf_op jit(solution)/shard_map/pallas_call | solution.py:329
  85.1 0.0 collective-permute-done
  85.1 0.0 collective-permute-done.1
  85.1 0.0 collective-permute-done.2
  85.1 0.0 copy-done
  85.2 0.8 add_convert_fusion
Async XLA Ops:
  60.8 24.4 %copy-start = (bf16[32,3072]{1,0:T(8,128)(2,1)S(1)}, bf16[32,3072]{1,0:T(8,128)(2,1)}, u32[]{:S(2)}) copy-start(bf16[32,3072]{1,0:T(8,128)(2,1)} %get-tuple-element.14) | copy-start | bytes 589828
  60.8 24.3 %collective-permute-start = (bf16[32,3072]{1,0:T(8,128)(2,1)}, bf16[32,3072]{1,0:T(8,128)(2,1)S(1)}, u32[]{:S(2)}, u32[]{:S(2)}) collective-permute-start(bf16[32,3072]{1,0:T(8,128)(2,1)} %get-tuple-element.15), channel_id=1, source_target_pairs={{0,4},{4,8},{8,12},{12,0},{1,5},{5,9},{9,13},{13,1},{2,6},{6,10},{... | collective-permute-start | bytes 589832 | tf_op jit(solution)/shard_map/ppermute | solution.py:325
  67.0 18.1 %collective-permute-start.1 = (bf16[32,3072]{1,0:T(8,128)(2,1)}, bf16[32,3072]{1,0:T(8,128)(2,1)S(1)}, u32[]{:S(2)}, u32[]{:S(2)}) collective-permute-start(bf16[32,3072]{1,0:T(8,128)(2,1)} %get-tuple-element.16), channel_id=1, source_target_pairs={{0,8},{4,12},{8,0},{12,4},{1,9},{5,13},{9,1},{13,5},{2,10},{6,14},... | collective-permute-start | bytes 589832 | tf_op jit(solution)/shard_map/ppermute | solution.py:325
  69.9 15.2 %collective-permute-start.2 = (bf16[32,3072]{1,0:T(8,128)(2,1)}, bf16[32,3072]{1,0:T(8,128)(2,1)S(1)}, u32[]{:S(2)}, u32[]{:S(2)}) collective-permute-start(bf16[32,3072]{1,0:T(8,128)(2,1)} %get-tuple-element.17), channel_id=1, source_target_pairs={{0,12},{4,0},{8,4},{12,8},{1,13},{5,1},{9,5},{13,9},{2,14},{6,2},{... | collective-permute-start | bytes 589832 | tf_op jit(solution)/shard_map/ppermute | solution.py:325
